TPU v7x, 256 devices: a whole 4x4x8 slice. The times are simulated.
256 devices in a mesh: lon: 32 (over z, x), lat: 2 (over core), head: 4 (over y).
Axes of the slice: x: 4, y: 4, z: 8, core: 2. Of those that a mesh axis runs over, the one named last changes fastest.
Arguments:
- queries: bfloat16 [32, 1280, 1024], P('lat', 'lon', 'head'), may hold values from -49 to 49
- keys: bfloat16 [32, 1280, 1024], P('lat', 'lon', 'head'), may hold values from -49 to 49
- values: bfloat16 [32, 1280, 1024], P('lat', 'lon', 'head'), may hold values from -16 to 16
- grad_out: bfloat16 [32, 1280, 1024], P('lat', 'lon', 'head'), may hold values from -64 to 64
- key_mask: int32 [32, 1280], P('lat', 'lon'), may hold values from 0 to 1
- offsets: int32 [4, 160], P('lat', 'lon'), may hold values from -8 to 8, as said below
- regions: int32 [4, 160], P('lat', 'lon'), may hold values from 0 to 7
Outputs:
- grad_queries: bfloat16 [32, 1280, 1024], P('lat', 'lon', 'head')
- grad_keys: bfloat16 [32, 1280, 1024], P('lat', 'lon', 'head')
- grad_values: bfloat16 [32, 1280, 1024], P('lat', 'lon', 'head')
Inputs may be any that keep to these rules, and one draw needn't show every extreme that they name: `offsets`: some block has offset -8 and some block has offset 8.
All inputs are finite; a program needn't handle non-finite values.
Results may differ from a plain program's by a relative error of at most 0.0095.
Values may be sent and summed in bfloat16 or wider, within the bound.
A program may use at most 64 MiB of HBM per device.

v0:
```python
import jax
import jax.numpy as jnp
from jax import lax
from jax.sharding import PartitionSpec as P

HS = 64
WIN = 8
REG_DEV = 8
MASKED_SCORE = -1e30


def extended_2(cells, sides, width):
    for axis, dim in sides:
        count = lax.axis_size(axis)
        head = lax.slice_in_dim(cells, 0, width, axis=dim)
        tail = lax.slice_in_dim(cells, cells.shape[dim] - width, cells.shape[dim], axis=dim)
        cells = jnp.concatenate(
            [
                lax.ppermute(tail, axis, [(i, (i + 1) % count) for i in range(count)]),
                cells,
                lax.ppermute(head, axis, [((i + 1) % count, i) for i in range(count)]),
            ],
            axis=dim,
        )
    return cells


def split_heads(array, head_count):
    return array.reshape(array.shape[:-1] + (head_count, HS))


def to_blocks(array):
    lat_cells, lon_cells = (array.shape[0], array.shape[1])
    trailing = array.shape[2:]
    grid_blocks = array.reshape((lat_cells // WIN, WIN, lon_cells // WIN, WIN) + trailing)
    perm_axes = (0, 2, 1, 3) + tuple(range(4, grid_blocks.ndim))
    return grid_blocks.transpose(perm_axes).reshape(
        (lat_cells // WIN, lon_cells // WIN, WIN * WIN) + trailing
    )


def from_blocks(array):
    lat_blocks, lon_blocks = (array.shape[0], array.shape[1])
    trailing = array.shape[3:]
    grid_blocks = array.reshape((lat_blocks, lon_blocks, WIN, WIN) + trailing)
    perm_axes = (0, 2, 1, 3) + tuple(range(4, grid_blocks.ndim))
    return grid_blocks.transpose(perm_axes).reshape((lat_blocks * WIN, lon_blocks * WIN) + trailing)


def window_blocks(extended, along):
    lon_blocks = extended.shape[1] - 4
    return jnp.concatenate([extended[:, step : step + lon_blocks] for step in range(5)], axis=along)


def fold_blocks(grads):
    cells = WIN * WIN
    folded = None
    for step in range(5):
        piece = grads[:, :, step * cells : (step + 1) * cells]
        piece = jnp.pad(piece, ((0, 0), (step, 4 - step), (0, 0), (0, 0)))
        folded = piece if folded is None else folded + piece
    return folded


def local(queries, keys, values, grad_out, key_mask, offsets, regions):
    highest = lax.Precision.HIGHEST
    lat_cells, lon_cells, features = queries.shape
    head_count = features // HS
    logit_scale = HS ** (-0.5)
    rim_blocks = 2
    cell_count = lat_cells * lon_cells
    lat_blocks, lon_blocks = (lat_cells // WIN, lon_cells // WIN)
    key_blocks = to_blocks(keys)
    value_blocks = to_blocks(values)
    query_blocks = to_blocks(queries)
    cotan_blocks = to_blocks(grad_out)
    mask_blocks = to_blocks(key_mask)
    block_region = jnp.broadcast_to(
        regions[:, :, None], (lat_blocks, lon_blocks, WIN * WIN)
    ).reshape(cell_count)
    weights = (block_region[:, None] == jnp.arange(REG_DEV, dtype=jnp.int32)[None, :]).astype(
        jnp.float32
    )
    weights = weights * mask_blocks.reshape(cell_count).astype(jnp.float32)[:, None]
    divisor = jnp.maximum(jnp.sum(weights, axis=0), 1.0)
    weights_low = weights.astype(jnp.bfloat16).T
    pooled_k = jnp.dot(
        weights_low, key_blocks.reshape(cell_count, features), preferred_element_type=jnp.float32
    )
    pooled_v = jnp.dot(
        weights_low, value_blocks.reshape(cell_count, features), preferred_element_type=jnp.float32
    )
    pooled = (jnp.stack([pooled_k, pooled_v], axis=1) / divisor[:, None, None]).astype(jnp.bfloat16)
    gathered = lax.all_gather(pooled, "lat", axis=0, tiled=True)
    reg_count = gathered.shape[0]
    register_key_rows = gathered[:, 0].reshape(reg_count, head_count, HS)
    register_value_rows = gathered[:, 1].reshape(reg_count, head_count, HS)
    key_ext, value_ext, mask_ext = (
        extended_2(key_blocks, (("lon", 1),), rim_blocks),
        extended_2(value_blocks, (("lon", 1),), rim_blocks),
        extended_2(mask_blocks, (("lon", 1),), rim_blocks),
    )
    cand_k = split_heads(window_blocks(key_ext, 2), head_count)
    candidate_values = split_heads(window_blocks(value_ext, 2), head_count)
    cand_mask = window_blocks(mask_ext, 2)
    key_offset = (
        jnp.arange(5, dtype=jnp.int32)[:, None, None] * WIN
        - 2 * WIN
        + jnp.zeros((1, WIN, 1), jnp.int32)
        + jnp.arange(WIN, dtype=jnp.int32)[None, None, :]
    ).reshape(5 * WIN * WIN)
    window_start = offsets[:, :, None]
    usable = (
        (key_offset >= window_start - WIN)
        & (key_offset < window_start + 2 * WIN)
        & (cand_mask == 1)
    )
    usable_b = usable[:, :, None, None, :]
    query_block = split_heads(query_blocks, head_count)
    gradient_block = split_heads(cotan_blocks, head_count)
    score_win = (
        jnp.einsum("abqhd,abkhd->abhqk", query_block, cand_k, preferred_element_type=jnp.float32)
        * logit_scale
    )
    score_win = jnp.where(usable_b, score_win, MASKED_SCORE)
    register_scores = (
        jnp.einsum(
            "abqhd,khd->abhqk", query_block, register_key_rows, preferred_element_type=jnp.float32
        )
        * logit_scale
    )
    row_max = jnp.maximum(jnp.max(score_win, axis=-1), jnp.max(register_scores, axis=-1))
    exp_total = jnp.sum(jnp.where(usable_b, jnp.exp(score_win - row_max[..., None]), 0.0), axis=-1)
    exp_total = exp_total + jnp.sum(jnp.exp(register_scores - row_max[..., None]), axis=-1)
    log_total = row_max + jnp.log(exp_total)
    prob_win = jnp.where(usable_b, jnp.exp(score_win - log_total[..., None]), 0.0)
    prob_reg = jnp.exp(register_scores - log_total[..., None])
    window_lower_bound = prob_win.astype(jnp.bfloat16)
    register_lower_bound = prob_reg.astype(jnp.bfloat16)
    attended_output = jnp.einsum(
        "abhqk,abkhd->abqhd",
        window_lower_bound,
        candidate_values,
        preferred_element_type=jnp.float32,
    )
    attended_output = attended_output + jnp.einsum(
        "abhqk,khd->abqhd",
        register_lower_bound,
        register_value_rows,
        preferred_element_type=jnp.float32,
    )
    delta_dot = jnp.sum(gradient_block.astype(jnp.float32) * attended_output, axis=-1)
    delta_heads = delta_dot.transpose(0, 1, 3, 2)
    dprob_win = jnp.einsum(
        "abqhd,abkhd->abhqk", gradient_block, candidate_values, preferred_element_type=jnp.float32
    )
    register_prob_gradient = jnp.einsum(
        "abqhd,khd->abhqk", gradient_block, register_value_rows, preferred_element_type=jnp.float32
    )
    dscore_win = (prob_win * (dprob_win - delta_heads[..., None])).astype(jnp.bfloat16)
    register_score_gradient = (prob_reg * (register_prob_gradient - delta_heads[..., None])).astype(
        jnp.bfloat16
    )
    grad_q = logit_scale * (
        jnp.einsum("abhqk,abkhd->abqhd", dscore_win, cand_k, preferred_element_type=jnp.float32)
        + jnp.einsum(
            "abhqk,khd->abqhd",
            register_score_gradient,
            register_key_rows,
            preferred_element_type=jnp.float32,
        )
    )
    grad_queries = from_blocks(grad_q.reshape(lat_blocks, lon_blocks, WIN * WIN, features)).astype(
        jnp.bfloat16
    )
    reg_grad_k = logit_scale * jnp.einsum(
        "abhqk,abqhd->khd", register_score_gradient, query_block, preferred_element_type=jnp.float32
    )
    reg_grad_v = jnp.einsum(
        "abhqk,abqhd->khd", register_lower_bound, gradient_block, preferred_element_type=jnp.float32
    )
    reg_grads = jnp.stack(
        [reg_grad_k.reshape(reg_count, features), reg_grad_v.reshape(reg_count, features)], axis=1
    )
    own_grads = lax.psum_scatter(
        reg_grads.astype(jnp.bfloat16), "lat", scatter_dimension=0, tiled=True
    ).astype(jnp.float32)
    spread = jnp.dot(
        weights,
        (own_grads / divisor[:, None, None]).reshape(REG_DEV, 2 * features),
        precision=highest,
    )
    spread = spread.reshape(lat_blocks, lon_blocks, WIN * WIN, 2 * features)
    grad_kc = logit_scale * jnp.einsum(
        "abhqk,abqhd->abkhd", dscore_win, query_block, preferred_element_type=jnp.float32
    )
    grad_vc = jnp.einsum(
        "abhqk,abqhd->abkhd", window_lower_bound, gradient_block, preferred_element_type=jnp.float32
    )
    ext_k = fold_blocks(grad_kc.reshape(grad_kc.shape[:3] + (features,)))
    ext_v = fold_blocks(grad_vc.reshape(grad_vc.shape[:3] + (features,)))
    edges_k = jnp.concatenate([ext_k[:, :rim_blocks], ext_k[:, -rim_blocks:]], axis=1)
    edges_v = jnp.concatenate([ext_v[:, :rim_blocks], ext_v[:, -rim_blocks:]], axis=1)
    got_k, got_v = (
        extended_2(edges_k, (("lon", 1),), rim_blocks),
        extended_2(edges_v, (("lon", 1),), rim_blocks),
    )
    win_k = ext_k[:, rim_blocks:-rim_blocks].at[:, :rim_blocks].add(got_k[:, :rim_blocks])
    win_k = win_k.at[:, -rim_blocks:].add(got_k[:, -rim_blocks:])
    win_v = ext_v[:, rim_blocks:-rim_blocks].at[:, :rim_blocks].add(got_v[:, :rim_blocks])
    win_v = win_v.at[:, -rim_blocks:].add(got_v[:, -rim_blocks:])
    grad_keys = from_blocks((win_k + spread[..., :features]).astype(jnp.bfloat16))
    grad_values = from_blocks((win_v + spread[..., features:]).astype(jnp.bfloat16))
    return (grad_queries, grad_keys, grad_values)


def solution(mesh):
    in_specs = (
        P("lat", "lon", "head"),
        P("lat", "lon", "head"),
        P("lat", "lon", "head"),
        P("lat", "lon", "head"),
        P("lat", "lon"),
        P("lat", "lon"),
        P("lat", "lon"),
    )
    out_specs = (P("lat", "lon", "head"), P("lat", "lon", "head"), P("lat", "lon", "head"))
    return jax.shard_map(local, mesh=mesh, in_specs=in_specs, out_specs=out_specs, check_vma=False)
```

profile of v0, /device:TPU:1, one launch (start us, length us, event | category | flops | bytes accessed | tf_op | source)
XLA Modules:
  0.0 155.2 jit_solution(9662106261121816254)
XLA Ops:
  8.1 2.1 %collective-permute-start.2 = (s32[2,2,64]{2,0,1:T(2,128)S(1)}, s32[2,2,64]{2,0,1:T(2,128)S(1)}, u32[]{:S(2)}, u32[]{:S(2)}) collective-permute-start(s32[2,2,64]{2,0,1:T(2,128)S(1)} %get-tuple-element.97), channel_id=1, source_target_pairs={{0,8},{8,16},{16,24},{24,32},{32,40},{40,48},{48,56},{56,64},{64,7... | collective-permute-start | bytes 3080 | tf_op jit(solution)/shard_map/ppermute | solution.py:19
  10.3 6.6 %collective-permute-start.3 = (s32[2,2,64]{2,0,1:T(2,128)S(1)}, s32[2,2,64]{2,0,1:T(2,128)S(1)}, u32[]{:S(2)}, u32[]{:S(2)}) collective-permute-start(s32[2,2,64]{2,0,1:T(2,128)S(1)} %get-tuple-element.96), channel_id=1, source_target_pairs={{8,0},{16,8},{24,16},{32,24},{40,32},{48,40},{56,48},{64,56},{72,6... | collective-permute-start | bytes 3080 | tf_op jit(solution)/shard_map/ppermute | solution.py:21
  21.8 4.7 %collective-permute-start.5 = (bf16[2,2,64,256]{3,2,1,0:T(8,128)(2,1)}, bf16[2,2,64,256]{3,2,1,0:T(8,128)(2,1)}, u32[]{:S(2)}, u32[]{:S(2)}) collective-permute-start(bf16[2,2,64,256]{3,2,1,0:T(8,128)(2,1)} %get-tuple-element.77), channel_id=1, source_target_pairs={{8,0},{16,8},{24,16},{32,24},{40,32},{48,40},{56,48},{64,56},{72,6... | collective-permute-start | bytes 393224 | tf_op jit(solution)/shard_map/ppermute | solution.py:21
  27.6 3.6 %all_gather.3 = bf16[16,2,256]{2,0,1:T(8,128)(2,1)S(1)} all-gather(bf16[8,2,256]{2,0,1:T(8,128)(2,1)S(1)} %fusion.51), channel_id=1, replica_groups=mesh['lon'=32,'lat'=2,'head'=4] {'lat'}, dimensions={0}, use_global_device_ids=true | all-gather | bytes 24576 | tf_op jit(solution)/shard_map/all_gather | solution.py:94
  44.7 4.1 %concatenate.77 = bf16[2,5,320,4,64]{2,4,3,1,0:T(8,128)(2,1)S(1)} concatenate(bf16[2,5,64,4,64]{2,4,3,1,0:T(8,128)(2,1)} %bitcast.189, bf16[2,5,64,4,64]{2,4,3,1,0:T(8,128)(2,1)} %bitcast.191, bf16[2,5,64,4,64]{2,4,3,1,0:T(8,128)(2,1)} %copy.410, bf16[2,5,64,4,64]{2,4,3,1,0:T(8,128)(2,1)} %bitcast.193, bf16[2,5,64,4,64]{2,4,3,1,0:T(8,128)(2,1)} %bitcast.195), dimensions={2} | concatenate | bytes 3276800 | tf_op jit(solution)/shard_map/concatenate | solution.py:52
  48.8 1.9 %bitcast_reduce_fusion = (f32[2,5,4,64]{3,2,1,0:T(4,128)S(1)}, f32[2,5,4,320,64]{3,4,2,1,0:T(8,128)S(1)}) fusion(pred[2,5,320]{2,1,0:T(8,128)(4,1)S(1)} %copy.416, bf16[2,5,64,4,64]{2,4,3,1,0:T(8,128)(2,1)} %copy.447, bf16[2,5,320,4,64]{2,4,3,1,0:T(8,128)(2,1)S(1)} %concatenate.77), kind=kOutput, calls=%fused_computation.4 | convolution fusion | flops 107312640 | bytes 5256320 | tf_op jit(solution)/shard_map/abqhd,abkhd->abhqk/dot_general | solution.py:122
  52.8 2.1 %pad_maximum_fusion = (bf16[2,5,64,256]{3,2,1,0:T(8,128)(2,1)}, bf16[2,5,64,256]{3,2,1,0:T(8,128)(2,1)}, bf16[2,5,64,256]{3,2,1,0:T(8,128)(2,1)}, bf16[2,5,64,256]{3,2,1,0:T(8,128)(2,1)}) fusion(bf16[2,2,64,256]{3,2,1,0:T(8,128)(2,1)} %collective-permute-done.5, bf16[2,5,64,256]{3,2,1,0:T(8,128)(2,1)S(1)} %bitcast.184, ...), kind=kLoop, calls=%fused_computation.62 | loop fusion | flops 655360 | bytes 1900544 | tf_op jit(solution)/shard_map/concatenate | solution.py:17
  54.9 2.2 %copy.428 = bf16[2,5,64,256]{2,3,1,0:T(8,128)(2,1)} copy(bf16[2,5,64,256]{3,2,1,0:T(8,128)(2,1)} %get-tuple-element.75) | data formatting | bytes 655360 | tf_op jit(solution)/shard_map/slice | solution.py:52
  57.0 2.0 %copy.429 = bf16[2,5,64,256]{2,3,1,0:T(8,128)(2,1)} copy(bf16[2,5,64,256]{3,2,1,0:T(8,128)(2,1)} %get-tuple-element.76) | data formatting | bytes 655360 | tf_op jit(solution)/shard_map/slice | solution.py:52
  59.1 2.1 %copy.431 = bf16[2,5,64,256]{2,3,1,0:T(8,128)(2,1)} copy(bf16[2,5,64,256]{3,2,1,0:T(8,128)(2,1)} %get-tuple-element.68) | data formatting | bytes 655360 | tf_op jit(solution)/shard_map/slice | solution.py:52
  63.7 5.3 %concatenate.88 = bf16[2,5,320,4,64]{2,4,3,1,0:T(8,128)(2,1)} concatenate(bf16[2,5,64,4,64]{2,4,3,1,0:T(8,128)(2,1)} %bitcast.188, bf16[2,5,64,4,64]{2,4,3,1,0:T(8,128)(2,1)} %bitcast.190, bf16[2,5,64,4,64]{2,4,3,1,0:T(8,128)(2,1)} %copy.433, bf16[2,5,64,4,64]{2,4,3,1,0:T(8,128)(2,1)} %bitcast.192, bf16[2,5,64,4,64]{2,4,3,1,0:T(8,128)(2,1)} %bitcast.194), dimensions={2} | concatenate | bytes 3276800 | tf_op jit(solution)/shard_map/concatenate | solution.py:52
  69.0 4.5 %fusion.12 = f32[2,5,64,4]{2,3,1,0:T(4,128)S(1)} fusion(f32[2,5,64,4,64]{2,4,3,1,0:T(8,128)} %convolution_bitcast_fusion.3, bf16[2,5,320,4,64]{2,4,3,1,0:T(8,128)(2,1)} %concatenate.88, bf16[2,5,64,4,64]{2,4,3,1,0:T(8,128)(2,1)S(1)} %copy-done.27, f32[2,5,4,320,64]{3,4,2,1,0:T(8,128)} %copy-done, f32[2,5,4,64]{3,2,1,0:T(4,128)S(1)} %fusion.47, ...), kind=kOutput, calls=%fused_computation.22 | convolution fusion | flops 109606400 | bytes 5921920 | tf_op jit(solution)/shard_map/abhqk,abkhd->abqhd/dot_general | solution.py:140
  73.9 2.7 %fusion = bf16[2,5,4,64,320]{4,3,2,1,0:T(8,128)(2,1)} fusion(f32[2,5,4,320,64]{3,4,2,1,0:T(8,128)S(1)} %copy-done.1, bf16[2,5,64,4,64]{2,4,3,1,0:T(8,128)(2,1)S(1)} %copy-done.27, bf16[2,5,320,4,64]{2,4,3,1,0:T(8,128)(2,1)S(1)} %copy-done.28, f32[2,5,4,64]{3,2,1,0:T(4,128)S(1)} %bitcast.214, f32[2,5,4,64]{3,2,1,0:T(4,128)S(1)} %fusion.47, ...), kind=kOutput, calls=%fused_computation.1 | convolution fusion | flops 110592000 | bytes 6904960 | tf_op jit(solution)/shard_map/abqhd,abkhd->abhqk/dot_general | solution.py:154
  77.9 3.6 %fusion.68 = (f32[2,5,64,256]{2,3,1,0:T(8,128)}, f32[2,5,64,256]{2,3,1,0:T(8,128)}, f32[2,5,64,256]{2,3,1,0:T(8,128)}, f32[2,5,64,256]{2,3,1,0:T(8,128)}, f32[2,5,64,256]{2,3,1,0:T(8,128)}) fusion(f32[2,5,320,256]{2,3,1,0:T(8,128)S(1)} %bitcast.181), kind=kLoop, calls=%fused_computation.132 | loop fusion | bytes 6553600 | tf_op jit(solution)/shard_map/slice | solution.py:59
  81.5 1.7 %copy.497 = f32[2,5,64,256]{3,2,1,0:T(8,128)S(1)} copy(f32[2,5,64,256]{2,3,1,0:T(8,128)} %get-tuple-element.55) | data formatting | bytes 1310720
  83.2 2.5 %copy.496 = f32[2,5,64,256]{3,2,1,0:T(8,128)} copy(f32[2,5,64,256]{2,3,1,0:T(8,128)} %get-tuple-element.52) | data formatting | bytes 1310720
  85.8 2.6 %copy.495 = f32[2,5,64,256]{3,2,1,0:T(8,128)} copy(f32[2,5,64,256]{2,3,1,0:T(8,128)} %get-tuple-element.53) | data formatting | bytes 1310720
  88.3 2.6 %copy.494 = f32[2,5,64,256]{3,2,1,0:T(8,128)} copy(f32[2,5,64,256]{2,3,1,0:T(8,128)} %get-tuple-element.54) | data formatting | bytes 1310720
  90.9 2.5 %copy.493 = f32[2,5,64,256]{3,2,1,0:T(8,128)} copy(f32[2,5,64,256]{2,3,1,0:T(8,128)} %get-tuple-element.51) | data formatting | bytes 1310720
  93.5 3.1 %pad_add_fusion = f32[2,9,64,256]{3,2,1,0:T(8,128)} fusion(f32[2,5,64,256]{3,2,1,0:T(8,128)S(1)} %copy.497, f32[2,5,64,256]{3,2,1,0:T(8,128)} %copy.496, f32[2,5,64,256]{3,2,1,0:T(8,128)} %copy.495, f32[2,5,64,256]{3,2,1,0:T(8,128)} %copy.494, f32[2,5,64,256]{3,2,1,0:T(8,128)} %copy.493), kind=kLoop, calls=%fused_computation.28 | loop fusion | flops 1179648 | bytes 4456448 | tf_op jit(solution)/shard_map/add | solution.py:61
  99.6 2.5 %convolution_multiply_fusion = f32[2,5,4,320,64]{3,4,2,1,0:T(8,128)} fusion(bf16[2,5,64,4,64]{2,4,3,1,0:T(8,128)(2,1)S(1)} %copy-done.23, bf16[2,5,4,64,320]{4,3,2,1,0:T(8,128)(2,1)S(1)} %copy-done.22), kind=kOutput, calls=%fused_computation.12 | convolution fusion | flops 105676800 | bytes 5242880 | tf_op jit(solution)/shard_map/abhqk,abqhd->abkhd/dot_general | solution.py:194
  104.6 6.2 %fusion.69 = (f32[2,5,64,256]{2,3,1,0:T(8,128)}, f32[2,5,64,256]{2,3,1,0:T(8,128)S(1)}, f32[2,5,64,256]{2,3,1,0:T(8,128)}, f32[2,5,64,256]{2,3,1,0:T(8,128)}, f32[2,5,64,256]{2,3,1,0:T(8,128)}) fusion(f32[2,5,320,256]{2,3,1,0:T(8,128)} %bitcast.180), kind=kLoop, calls=%fused_computation.133 | loop fusion | bytes 6553600 | tf_op jit(solution)/shard_map/slice | solution.py:59
  110.8 1.7 %copy.492 = f32[2,5,64,256]{3,2,1,0:T(8,128)S(1)} copy(f32[2,5,64,256]{2,3,1,0:T(8,128)} %get-tuple-element.60) | data formatting | bytes 1310720
  112.9 1.9 %copy.490 = f32[2,5,64,256]{3,2,1,0:T(8,128)S(1)} copy(f32[2,5,64,256]{2,3,1,0:T(8,128)} %get-tuple-element.58) | data formatting | bytes 1310720
  114.8 1.9 %copy.489 = f32[2,5,64,256]{3,2,1,0:T(8,128)S(1)} copy(f32[2,5,64,256]{2,3,1,0:T(8,128)} %get-tuple-element.59) | data formatting | bytes 1310720
  116.8 2.8 %copy.488 = f32[2,5,64,256]{3,2,1,0:T(8,128)} copy(f32[2,5,64,256]{2,3,1,0:T(8,128)} %get-tuple-element.56) | data formatting | bytes 1310720
  119.6 2.4 %pad_add_fusion.1 = f32[2,9,64,256]{3,2,1,0:T(8,128)} fusion(f32[2,5,64,256]{3,2,1,0:T(8,128)S(1)} %copy.492, f32[2,5,64,256]{3,2,1,0:T(8,128)S(1)} %copy.491, f32[2,5,64,256]{3,2,1,0:T(8,128)S(1)} %copy.490, f32[2,5,64,256]{3,2,1,0:T(8,128)S(1)} %copy.489, f32[2,5,64,256]{3,2,1,0:T(8,128)} %copy.488), kind=kLoop, calls=%fused_computation.29 | loop fusion | flops 1179648 | bytes 4456448 | tf_op jit(solution)/shard_map/add | solution.py:61
  125.5 2.1 %slice.319 = f32[2,5,64,256]{3,2,1,0:T(8,128)} slice(f32[2,9,64,256]{3,2,1,0:T(8,128)} %pad_add_fusion), slice={[0:2], [2:7], [0:64], [0:256]} | slice | bytes 1310720 | tf_op jit(solution)/shard_map/slice | solution.py:210
  127.6 4.8 %collective-permute-start.9 = (f32[2,2,64,256]{3,2,1,0:T(8,128)}, f32[2,2,64,256]{3,2,1,0:T(8,128)S(1)}, u32[]{:S(2)}, u32[]{:S(2)}) collective-permute-start(f32[2,2,64,256]{3,2,1,0:T(8,128)} %get-tuple-element.61), channel_id=1, source_target_pairs={{8,0},{16,8},{24,16},{32,24},{40,32},{48,40},{56,48},{64,56},{72,6... | collective-permute-start | bytes 786440 | tf_op jit(solution)/shard_map/ppermute | solution.py:21
  132.4 4.8 %collective-permute-start.7 = (f32[2,2,64,256]{3,2,1,0:T(8,128)}, f32[2,2,64,256]{3,2,1,0:T(8,128)}, u32[]{:S(2)}, u32[]{:S(2)}) collective-permute-start(f32[2,2,64,256]{3,2,1,0:T(8,128)} %get-tuple-element.63), channel_id=1, source_target_pairs={{8,0},{16,8},{24,16},{32,24},{40,32},{48,40},{56,48},{64,56},{72,6... | collective-permute-start | bytes 786440 | tf_op jit(solution)/shard_map/ppermute | solution.py:21
  139.5 1.9 %fusion.36 = f32[2,5,64,256]{3,2,1,0:T(8,128)} fusion(f32[2,5,64,256]{3,2,1,0:T(8,128)} %slice.319, f32[2,2,64,256]{3,2,1,0:T(8,128)} %collective-permute-done.8, f32[2,5,64,256]{3,2,1,0:T(8,128)S(1)} %copy.497, f32[2,5,64,256]{3,2,1,0:T(8,128)S(1)} %copy-done.3, f32[2,5,64,256]{3,2,1,0:T(8,128)S(1)} %copy-done.5, f32[2,5,64,256]{3,2,1,0:T(8,128)S(1)} %copy-done.7, ...), kind=kLoop, calls=%fused_computation.76 | loop fusion | flops 327680 | bytes 3801088 | tf_op jit(solution)/shard_map/scatter-add | solution.py:210
  141.4 3.1 %collective-permute-done.6 = f32[2,2,64,256]{3,2,1,0:T(8,128)} collective-permute-done((f32[2,2,64,256]{3,2,1,0:T(8,128)}, f32[2,2,64,256]{3,2,1,0:T(8,128)}, u32[]{:S(2)}, u32[]{:S(2)}) %collective-permute-start.6) | collective-permute-done | bytes 262176 | tf_op jit(solution)/shard_map/ppermute | solution.py:19
  (171 shorter events, 41.8 us)
Async XLA Ops:
  7.2 19.3 %copy-start.30 = (bf16[16,40,256]{2,1,0:T(8,128)(2,1)S(1)}, bf16[16,40,256]{2,1,0:T(8,128)(2,1)}, u32[]{:S(2)}) copy-start(bf16[16,40,256]{2,1,0:T(8,128)(2,1)} %param.15) | copy-start | bytes 983044
  7.2 130.0 %reduce-scatter.4.cloned.1.call-start = ((), (), s32[]{:S(2)}) async-start(), calls=%async_computation.1 | async-start | bytes 24576
  8.1 30.8 %collective-permute-start.2 = (s32[2,2,64]{2,0,1:T(2,128)S(1)}, s32[2,2,64]{2,0,1:T(2,128)S(1)}, u32[]{:S(2)}, u32[]{:S(2)}) collective-permute-start(s32[2,2,64]{2,0,1:T(2,128)S(1)} %get-tuple-element.97), channel_id=1, source_target_pairs={{0,8},{8,16},{16,24},{24,32},{32,40},{40,48},{48,56},{56,64},{64,7... | collective-permute-start | bytes 3080 | tf_op jit(solution)/shard_map/ppermute | solution.py:19
  10.3 28.7 %collective-permute-start.3 = (s32[2,2,64]{2,0,1:T(2,128)S(1)}, s32[2,2,64]{2,0,1:T(2,128)S(1)}, u32[]{:S(2)}, u32[]{:S(2)}) collective-permute-start(s32[2,2,64]{2,0,1:T(2,128)S(1)} %get-tuple-element.96), channel_id=1, source_target_pairs={{8,0},{16,8},{24,16},{32,24},{40,32},{48,40},{56,48},{64,56},{72,6... | collective-permute-start | bytes 3080 | tf_op jit(solution)/shard_map/ppermute | solution.py:21
  16.9 10.0 %copy-start.31 = (s32[2,5]{1,0:T(2,128)S(1)}, s32[2,5]{1,0:T(2,128)}, u32[]{:S(2)}) copy-start(s32[2,5]{1,0:T(2,128)} %param.21) | copy-start | bytes 124
  18.6 20.6 %collective-permute-start.1 = (bf16[2,2,64,256]{3,2,1,0:T(8,128)(2,1)}, bf16[2,2,64,256]{3,2,1,0:T(8,128)(2,1)}, u32[]{:S(2)}, u32[]{:S(2)}) collective-permute-start(bf16[2,2,64,256]{3,2,1,0:T(8,128)(2,1)} %get-tuple-element.83), channel_id=1, source_target_pairs={{8,0},{16,8},{24,16},{32,24},{40,32},{48,40},{56,48},{64,56},{72,6... | collective-permute-start | bytes 393224 | tf_op jit(solution)/shard_map/ppermute | solution.py:21
  20.0 19.2 %collective-permute-start = (bf16[2,2,64,256]{3,2,1,0:T(8,128)(2,1)}, bf16[2,2,64,256]{3,2,1,0:T(8,128)(2,1)}, u32[]{:S(2)}, u32[]{:S(2)}) collective-permute-start(bf16[2,2,64,256]{3,2,1,0:T(8,128)(2,1)} %get-tuple-element.84), channel_id=1, source_target_pairs={{0,8},{8,16},{16,24},{24,32},{32,40},{40,48},{48,56},{56,64},{64,7... | collective-permute-start | bytes 393224 | tf_op jit(solution)/shard_map/ppermute | solution.py:19
  21.8 10.2 %copy-start.32 = (s32[2,5]{1,0:T(2,128)S(1)}, s32[2,5]{1,0:T(2,128)}, u32[]{:S(2)}) copy-start(s32[2,5]{1,0:T(2,128)} %param.20) | copy-start | bytes 124
  21.8 31.0 %collective-permute-start.5 = (bf16[2,2,64,256]{3,2,1,0:T(8,128)(2,1)}, bf16[2,2,64,256]{3,2,1,0:T(8,128)(2,1)}, u32[]{:S(2)}, u32[]{:S(2)}) collective-permute-start(bf16[2,2,64,256]{3,2,1,0:T(8,128)(2,1)} %get-tuple-element.77), channel_id=1, source_target_pairs={{8,0},{16,8},{24,16},{32,24},{40,32},{48,40},{56,48},{64,56},{72,6... | collective-permute-start | bytes 393224 | tf_op jit(solution)/shard_map/ppermute | solution.py:21
  26.8 6.6 %copy-start.24 = (bf16[2,5,64,4,64]{4,3,2,1,0:T(4,128)(2,1)}, bf16[2,5,64,4,64]{4,3,2,1,0:T(4,128)(2,1)S(1)}, u32[]{:S(2)}) copy-start(bf16[2,5,64,4,64]{4,3,2,1,0:T(4,128)(2,1)S(1)} %reshape_reshape.14) | copy-start | bytes 983044
  32.0 30.3 %copy-start.20 = (f32[2,5,4,64,16]{3,4,1,0,2:T(8,128)}, f32[2,5,4,64,16]{3,4,1,0,2:T(8,128)S(1)}, u32[]{:S(2)}) copy-start(f32[2,5,4,64,16]{3,4,1,0,2:T(8,128)S(1)} %get-tuple-element.103) | copy-start | bytes 491524
  38.9 13.9 %collective-permute-start.4 = (bf16[2,2,64,256]{3,2,1,0:T(8,128)(2,1)S(1)}, bf16[2,2,64,256]{3,2,1,0:T(8,128)(2,1)}, u32[]{:S(2)}, u32[]{:S(2)}) collective-permute-start(bf16[2,2,64,256]{3,2,1,0:T(8,128)(2,1)S(1)} %get-tuple-element.78), channel_id=1, source_target_pairs={{0,8},{8,16},{16,24},{24,32},{32,40},{40,48},{48,56},{56,64},{64,7... | collective-permute-start | bytes 393224 | tf_op jit(solution)/shard_map/ppermute | solution.py:19
  54.9 6.3 %copy-start.29 = (bf16[2,5,64,256]{3,2,1,0:T(8,128)(2,1)S(1)}, bf16[2,5,64,256]{3,2,1,0:T(8,128)(2,1)}, u32[]{:S(2)}) copy-start(bf16[2,5,64,256]{3,2,1,0:T(8,128)(2,1)} %get-tuple-element.67) | copy-start | bytes 983044
  63.7 5.3 %copy-start.27 = (bf16[2,5,64,4,64]{2,4,3,1,0:T(8,128)(2,1)S(1)}, bf16[2,5,64,4,64]{2,4,3,1,0:T(8,128)(2,1)}, u32[]{:S(2)}) copy-start(bf16[2,5,64,4,64]{2,4,3,1,0:T(8,128)(2,1)} %copy.436) | copy-start | bytes 983044
  112.5 9.5 %copy-start.10 = (f32[2,5,64,256]{3,2,1,0:T(8,128)}, f32[2,5,64,256]{3,2,1,0:T(8,128)S(1)}, u32[]{:S(2)}) copy-start(f32[2,5,64,256]{3,2,1,0:T(8,128)S(1)} %copy.492) | copy-start | bytes 1966084
  112.9 9.1 %copy-start.12 = (f32[2,5,64,256]{3,2,1,0:T(8,128)}, f32[2,5,64,256]{3,2,1,0:T(8,128)S(1)}, u32[]{:S(2)}) copy-start(f32[2,5,64,256]{3,2,1,0:T(8,128)S(1)} %copy.491) | copy-start | bytes 1966084
  114.8 7.2 %copy-start.14 = (f32[2,5,64,256]{3,2,1,0:T(8,128)}, f32[2,5,64,256]{3,2,1,0:T(8,128)S(1)}, u32[]{:S(2)}) copy-start(f32[2,5,64,256]{3,2,1,0:T(8,128)S(1)} %copy.490) | copy-start | bytes 1966084
  116.8 5.2 %copy-start.16 = (f32[2,5,64,256]{3,2,1,0:T(8,128)}, f32[2,5,64,256]{3,2,1,0:T(8,128)S(1)}, u32[]{:S(2)}) copy-start(f32[2,5,64,256]{3,2,1,0:T(8,128)S(1)} %copy.489) | copy-start | bytes 1966084
  125.5 14.0 %copy-start.3 = (f32[2,5,64,256]{3,2,1,0:T(8,128)S(1)}, f32[2,5,64,256]{3,2,1,0:T(8,128)}, u32[]{:S(2)}) copy-start(f32[2,5,64,256]{3,2,1,0:T(8,128)} %copy.496) | copy-start | bytes 1966084
  125.5 14.0 %copy-start.5 = (f32[2,5,64,256]{3,2,1,0:T(8,128)S(1)}, f32[2,5,64,256]{3,2,1,0:T(8,128)}, u32[]{:S(2)}) copy-start(f32[2,5,64,256]{3,2,1,0:T(8,128)} %copy.495) | copy-start | bytes 1966084
  125.5 14.0 %copy-start.7 = (f32[2,5,64,256]{3,2,1,0:T(8,128)S(1)}, f32[2,5,64,256]{3,2,1,0:T(8,128)}, u32[]{:S(2)}) copy-start(f32[2,5,64,256]{3,2,1,0:T(8,128)} %copy.494) | copy-start | bytes 1966084
  125.5 14.0 %copy-start.9 = (f32[2,5,64,256]{3,2,1,0:T(8,128)S(1)}, f32[2,5,64,256]{3,2,1,0:T(8,128)}, u32[]{:S(2)}) copy-start(f32[2,5,64,256]{3,2,1,0:T(8,128)} %copy.493) | copy-start | bytes 1966084
  127.6 11.8 %collective-permute-start.8 = (f32[2,2,64,256]{3,2,1,0:T(8,128)}, f32[2,2,64,256]{3,2,1,0:T(8,128)}, u32[]{:S(2)}, u32[]{:S(2)}) collective-permute-start(f32[2,2,64,256]{3,2,1,0:T(8,128)} %get-tuple-element.62), channel_id=1, source_target_pairs={{0,8},{8,16},{16,24},{24,32},{32,40},{40,48},{48,56},{56,64},{64,7... | collective-permute-start | bytes 786440 | tf_op jit(solution)/shard_map/ppermute | solution.py:19
  127.6 17.9 %collective-permute-start.9 = (f32[2,2,64,256]{3,2,1,0:T(8,128)}, f32[2,2,64,256]{3,2,1,0:T(8,128)S(1)}, u32[]{:S(2)}, u32[]{:S(2)}) collective-permute-start(f32[2,2,64,256]{3,2,1,0:T(8,128)} %get-tuple-element.61), channel_id=1, source_target_pairs={{8,0},{16,8},{24,16},{32,24},{40,32},{48,40},{56,48},{64,56},{72,6... | collective-permute-start | bytes 786440 | tf_op jit(solution)/shard_map/ppermute | solution.py:21
  132.4 12.0 %collective-permute-start.6 = (f32[2,2,64,256]{3,2,1,0:T(8,128)}, f32[2,2,64,256]{3,2,1,0:T(8,128)}, u32[]{:S(2)}, u32[]{:S(2)}) collective-permute-start(f32[2,2,64,256]{3,2,1,0:T(8,128)} %get-tuple-element.64), channel_id=1, source_target_pairs={{0,8},{8,16},{16,24},{24,32},{32,40},{40,48},{48,56},{56,64},{64,7... | collective-permute-start | bytes 786440 | tf_op jit(solution)/shard_map/ppermute | solution.py:19
  132.4 13.2 %collective-permute-start.7 = (f32[2,2,64,256]{3,2,1,0:T(8,128)}, f32[2,2,64,256]{3,2,1,0:T(8,128)}, u32[]{:S(2)}, u32[]{:S(2)}) collective-permute-start(f32[2,2,64,256]{3,2,1,0:T(8,128)} %get-tuple-element.63), channel_id=1, source_target_pairs={{8,0},{16,8},{24,16},{32,24},{40,32},{48,40},{56,48},{64,56},{72,6... | collective-permute-start | bytes 786440 | tf_op jit(solution)/shard_map/ppermute | solution.py:21
  138.0 6.5 %slice-start = ((f32[2,9,64,256]{3,2,1,0:T(8,128)}), f32[2,5,64,256]{3,2,1,0:T(8,128)S(1)}, s32[]{:S(2)}) async-start(f32[2,9,64,256]{3,2,1,0:T(8,128)} %pad_add_fusion.1), calls=%async_computation.2 | async-start | bytes 1310720 | tf_op jit(solution)/shard_map/slice | solution.py:208
  139.4 5.1 %copy-start.11 = (f32[2,5,64,256]{3,2,1,0:T(8,128)S(1)}, f32[2,5,64,256]{3,2,1,0:T(8,128)}, u32[]{:S(2)}) copy-start(f32[2,5,64,256]{3,2,1,0:T(8,128)} %copy-done.10) | copy-start | bytes 1966084
  139.4 5.1 %copy-start.13 = (f32[2,5,64,256]{3,2,1,0:T(8,128)S(1)}, f32[2,5,64,256]{3,2,1,0:T(8,128)}, u32[]{:S(2)}) copy-start(f32[2,5,64,256]{3,2,1,0:T(8,128)} %copy-done.12) | copy-start | bytes 1966084
  139.4 5.1 %copy-start.15 = (f32[2,5,64,256]{3,2,1,0:T(8,128)S(1)}, f32[2,5,64,256]{3,2,1,0:T(8,128)}, u32[]{:S(2)}) copy-start(f32[2,5,64,256]{3,2,1,0:T(8,128)} %copy-done.14) | copy-start | bytes 1966084
  139.4 5.1 %copy-start.17 = (f32[2,5,64,256]{3,2,1,0:T(8,128)S(1)}, f32[2,5,64,256]{3,2,1,0:T(8,128)}, u32[]{:S(2)}) copy-start(f32[2,5,64,256]{3,2,1,0:T(8,128)} %copy-done.16) | copy-start | bytes 1966084
  139.4 5.1 %copy-start.19 = (f32[2,5,64,256]{3,2,1,0:T(8,128)S(1)}, f32[2,5,64,256]{3,2,1,0:T(8,128)}, u32[]{:S(2)}) copy-start(f32[2,5,64,256]{3,2,1,0:T(8,128)} %copy.488) | copy-start | bytes 1966084
  (13 other events, 36.0 us)
Sparse Core Ops, SparseCore 0:
  104.7 11.7 reduce-scatter.3
where the time goes:
time: 156 us; the launch traced here: 155 us
  local copies, waits for them, and re-layouts  72 us (46%)
  starting transfers between devices  24.5 us (16%)
  matrix products  20 us (13%)
  other arithmetic  17.2 us (11%)
  between operations  14.7 us (9%)
  blocking collectives  3.59 us (2%)
  waiting for transfers between devices  3.11 us (2%)
    unnamed x78, local copies, waits for them, and re-layouts  22.7 us
    ppermute x5, starting transfers between devices, extended_2(): lax.ppermute(head, axis, [((i + 1) % count, i) for i in range(count)])  22.3 us
    concatenate x7, local copies, waits for them, and re-layouts, window_blocks(): jnp.concatenate([extended[:, step:step + lon_blocks] for step in range(5)...  12.5 us
    slice x10, local copies, waits for them, and re-layouts, window_blocks(): extended[:, step:step + lon_blocks]  11.8 us
    slice x2, local copies, waits for them, and re-layouts, fold_blocks(): piece = grads[:, :, step * cells:(step + 1) * cells]  9.79 us
    add x2, other arithmetic, fold_blocks(): folded = piece if folded is None else folded + piece  5.51 us
    dot_general x1, matrix products, local(): jnp.einsum('abhqk,abkhd->abqhd', window_lower_bound, candidate_values, pr...  4.53 us
    all_gather x1, blocking collectives, local(): gathered = lax.all_gather(pooled, 'lat', axis=0, tiled=True)  3.59 us
  transfers between devices with their start and end apart: 11, of which 1 were waited for; matrix products, arithmetic and copies ran while one was open for 34% of the time, Pallas kernels for 0%

commit v1 on v0

--- a/solution.py
+++ b/solution.py
@@ -91,7 +91,9 @@
         weights_low, value_blocks.reshape(cell_count, features), preferred_element_type=jnp.float32
     )
     pooled = (jnp.stack([pooled_k, pooled_v], axis=1) / divisor[:, None, None]).astype(jnp.bfloat16)
-    gathered = lax.all_gather(pooled, "lat", axis=0, tiled=True)
+    gathered = jnp.concatenate(
+        lax.all_to_all(jnp.stack([pooled] * lax.axis_size("lat")), "lat", 0, 0), axis=0
+    )
     reg_count = gathered.shape[0]
     register_key_rows = gathered[:, 0].reshape(reg_count, head_count, HS)
     register_value_rows = gathered[:, 1].reshape(reg_count, head_count, HS)

time: 156 us -> 158 us (1.013)
  starting transfers between devices: 24.5 us -> 28.4 us
  blocking collectives: 3.59 us -> 0 us
    all_to_all x0 -> x1, starting transfers between devices: none -> 6.47 us  [local(): lax.all_to_all(jnp.stack([pooled] * lax.axis_size('lat')), 'lat', 0, 0)]
    all_gather x1 -> x0, blocking collectives: 3.59 us -> none  [local(): gathered = lax.all_gather(pooled, 'lat', axis=0, tiled=True)]
    ppermute x5, starting transfers between devices: 2.22 us -> 0.18 us  [extended_2(): lax.ppermute(tail, axis, [(i, (i + 1) % count) for i in range(count)])]
  transfers between devices with their start and end apart: 11 -> 12, of which waited for: 1 -> 1; matrix products, arithmetic and copies ran while one was open for 34% -> 32% of each run, Pallas kernels for 0% -> 0%
where the time goes in v1:
time: 158 us; the launch traced here: 156 us
  local copies, waits for them, and re-layouts  72.7 us (46%)
  starting transfers between devices  28.4 us (18%)
  matrix products  20 us (13%)
  other arithmetic  17.9 us (11%)
  between operations  14.8 us (9%)
  waiting for transfers between devices  2.15 us (1%)
    unnamed x78, local copies, waits for them, and re-layouts  22.8 us
    ppermute x5, starting transfers between devices, extended_2(): lax.ppermute(head, axis, [((i + 1) % count, i) for i in range(count)])  21.7 us
    concatenate x7, local copies, waits for them, and re-layouts, window_blocks(): jnp.concatenate([extended[:, step:step + lon_blocks] for step in range(5)...  12.4 us
    slice x10, local copies, waits for them, and re-layouts, window_blocks(): extended[:, step:step + lon_blocks]  11.8 us
    slice x2, local copies, waits for them, and re-layouts, fold_blocks(): piece = grads[:, :, step * cells:(step + 1) * cells]  9.75 us
    all_to_all x1, starting transfers between devices, local(): lax.all_to_all(jnp.stack([pooled] * lax.axis_size('lat')), 'lat', 0, 0)  6.47 us
    add x2, other arithmetic, fold_blocks(): folded = piece if folded is None else folded + piece  5.49 us
    dot_general x1, matrix products, local(): jnp.einsum('abhqk,abkhd->abqhd', window_lower_bound, candidate_values, pr...  4.53 us
  transfers between devices with their start and end apart: 12, of which 1 were waited for; matrix products, arithmetic and copies ran while one was open for 32% of the time, Pallas kernels for 0%

profile of v1, /device:TPU:1, one launch (start us, length us, event | category | flops | bytes accessed | tf_op | source)
XLA Modules:
  0.0 155.9 jit_solution(14045355742687686868)
XLA Ops:
  12.1 6.5 %all-to-all-start = ((bf16[2,8,2,256]{3,1,2,0:T(8,128)(2,1)}), bf16[2,8,2,256]{3,1,2,0:T(8,128)(2,1)S(1)}, u32[]{:S(2)}, u32[]{:S(2)}) async-start(bf16[2,8,2,256]{3,1,2,0:T(8,128)(2,1)} %pad_maximum_fusion.4), calls=%async_computation | async-start | bytes 32768 | tf_op jit(solution)/shard_map/all_to_all | solution.py:95
  18.8 6.1 %collective-permute-start.3 = (s32[2,2,64]{2,0,1:T(2,128)S(1)}, s32[2,2,64]{2,0,1:T(2,128)S(1)}, u32[]{:S(2)}, u32[]{:S(2)}) collective-permute-start(s32[2,2,64]{2,0,1:T(2,128)S(1)} %get-tuple-element.96), channel_id=1, source_target_pairs={{8,0},{16,8},{24,16},{32,24},{40,32},{48,40},{56,48},{64,56},{72,6... | collective-permute-start | bytes 3080 | tf_op jit(solution)/shard_map/ppermute | solution.py:21
  27.7 4.7 %collective-permute-start.5 = (bf16[2,2,64,256]{3,2,1,0:T(8,128)(2,1)}, bf16[2,2,64,256]{3,2,1,0:T(8,128)(2,1)}, u32[]{:S(2)}, u32[]{:S(2)}) collective-permute-start(bf16[2,2,64,256]{3,2,1,0:T(8,128)(2,1)} %get-tuple-element.77), channel_id=1, source_target_pairs={{8,0},{16,8},{24,16},{32,24},{40,32},{48,40},{56,48},{64,56},{72,6... | collective-permute-start | bytes 393224 | tf_op jit(solution)/shard_map/ppermute | solution.py:21
  46.3 4.1 %concatenate.84 = bf16[2,5,320,4,64]{2,4,3,1,0:T(8,128)(2,1)S(1)} concatenate(bf16[2,5,64,4,64]{2,4,3,1,0:T(8,128)(2,1)} %bitcast.192, bf16[2,5,64,4,64]{2,4,3,1,0:T(8,128)(2,1)} %bitcast.194, bf16[2,5,64,4,64]{2,4,3,1,0:T(8,128)(2,1)} %copy.349, bf16[2,5,64,4,64]{2,4,3,1,0:T(8,128)(2,1)} %bitcast.196, bf16[2,5,64,4,64]{2,4,3,1,0:T(8,128)(2,1)} %bitcast.198), dimensions={2} | concatenate | bytes 3276800 | tf_op jit(solution)/shard_map/concatenate | solution.py:52
  50.4 1.9 %bitcast_reduce_fusion = (f32[2,5,4,64]{3,2,1,0:T(4,128)S(1)}, f32[2,5,4,320,64]{3,4,2,1,0:T(8,128)S(1)}) fusion(pred[2,5,320]{2,1,0:T(8,128)(4,1)S(1)} %copy.355, bf16[2,5,64,4,64]{2,4,3,1,0:T(8,128)(2,1)} %copy.387, bf16[2,5,320,4,64]{2,4,3,1,0:T(8,128)(2,1)S(1)} %concatenate.84), kind=kOutput, calls=%fused_computation.4 | convolution fusion | flops 107312640 | bytes 5256320 | tf_op jit(solution)/shard_map/abqhd,abkhd->abhqk/dot_general | solution.py:124
  54.4 2.1 %pad_maximum_fusion = (bf16[2,5,64,256]{3,2,1,0:T(8,128)(2,1)}, bf16[2,5,64,256]{3,2,1,0:T(8,128)(2,1)}, bf16[2,5,64,256]{3,2,1,0:T(8,128)(2,1)}, bf16[2,5,64,256]{3,2,1,0:T(8,128)(2,1)}) fusion(bf16[2,2,64,256]{3,2,1,0:T(8,128)(2,1)} %collective-permute-done.5, bf16[2,5,64,256]{3,2,1,0:T(8,128)(2,1)S(1)} %bitcast.187, ...), kind=kLoop, calls=%fused_computation.62 | loop fusion | flops 655360 | bytes 1900544 | tf_op jit(solution)/shard_map/concatenate | solution.py:17
  56.5 2.2 %copy.368 = bf16[2,5,64,256]{2,3,1,0:T(8,128)(2,1)} copy(bf16[2,5,64,256]{3,2,1,0:T(8,128)(2,1)} %get-tuple-element.75) | data formatting | bytes 655360 | tf_op jit(solution)/shard_map/slice | solution.py:52
  58.6 2.1 %copy.369 = bf16[2,5,64,256]{2,3,1,0:T(8,128)(2,1)} copy(bf16[2,5,64,256]{3,2,1,0:T(8,128)(2,1)} %get-tuple-element.76) | data formatting | bytes 655360 | tf_op jit(solution)/shard_map/slice | solution.py:52
  60.7 2.1 %copy.371 = bf16[2,5,64,256]{2,3,1,0:T(8,128)(2,1)} copy(bf16[2,5,64,256]{3,2,1,0:T(8,128)(2,1)} %get-tuple-element.68) | data formatting | bytes 655360 | tf_op jit(solution)/shard_map/slice | solution.py:52
  65.4 5.3 %concatenate.95 = bf16[2,5,320,4,64]{2,4,3,1,0:T(8,128)(2,1)} concatenate(bf16[2,5,64,4,64]{2,4,3,1,0:T(8,128)(2,1)} %bitcast.191, bf16[2,5,64,4,64]{2,4,3,1,0:T(8,128)(2,1)} %bitcast.193, bf16[2,5,64,4,64]{2,4,3,1,0:T(8,128)(2,1)} %copy.373, bf16[2,5,64,4,64]{2,4,3,1,0:T(8,128)(2,1)} %bitcast.195, bf16[2,5,64,4,64]{2,4,3,1,0:T(8,128)(2,1)} %bitcast.197), dimensions={2} | concatenate | bytes 3276800 | tf_op jit(solution)/shard_map/concatenate | solution.py:52
  70.6 4.5 %fusion.12 = f32[2,5,64,4]{2,3,1,0:T(4,128)S(1)} fusion(f32[2,5,64,4,64]{2,4,3,1,0:T(8,128)} %convolution_bitcast_fusion.3, bf16[2,5,320,4,64]{2,4,3,1,0:T(8,128)(2,1)} %concatenate.95, bf16[2,5,64,4,64]{2,4,3,1,0:T(8,128)(2,1)S(1)} %copy-done.27, f32[2,5,4,320,64]{3,4,2,1,0:T(8,128)} %copy-done, f32[2,5,4,64]{3,2,1,0:T(4,128)S(1)} %fusion.47, ...), kind=kOutput, calls=%fused_computation.22 | convolution fusion | flops 109606400 | bytes 5921920 | tf_op jit(solution)/shard_map/abhqk,abkhd->abqhd/dot_general | solution.py:142
  75.5 2.7 %fusion = bf16[2,5,4,64,320]{4,3,2,1,0:T(8,128)(2,1)} fusion(f32[2,5,4,320,64]{3,4,2,1,0:T(8,128)S(1)} %copy-done.1, bf16[2,5,64,4,64]{2,4,3,1,0:T(8,128)(2,1)S(1)} %copy-done.27, bf16[2,5,320,4,64]{2,4,3,1,0:T(8,128)(2,1)S(1)} %copy-done.28, f32[2,5,4,64]{3,2,1,0:T(4,128)S(1)} %bitcast.218, f32[2,5,4,64]{3,2,1,0:T(4,128)S(1)} %fusion.47, ...), kind=kOutput, calls=%fused_computation.1 | convolution fusion | flops 110592000 | bytes 6904960 | tf_op jit(solution)/shard_map/abqhd,abkhd->abhqk/dot_general | solution.py:156
  79.5 3.6 %fusion.68 = (f32[2,5,64,256]{2,3,1,0:T(8,128)}, f32[2,5,64,256]{2,3,1,0:T(8,128)}, f32[2,5,64,256]{2,3,1,0:T(8,128)}, f32[2,5,64,256]{2,3,1,0:T(8,128)}, f32[2,5,64,256]{2,3,1,0:T(8,128)}) fusion(f32[2,5,320,256]{2,3,1,0:T(8,128)S(1)} %bitcast.184), kind=kLoop, calls=%fused_computation.134 | loop fusion | bytes 6553600 | tf_op jit(solution)/shard_map/slice | solution.py:59
  83.2 1.7 %copy.437 = f32[2,5,64,256]{3,2,1,0:T(8,128)S(1)} copy(f32[2,5,64,256]{2,3,1,0:T(8,128)} %get-tuple-element.55) | data formatting | bytes 1310720
  84.9 2.5 %copy.436 = f32[2,5,64,256]{3,2,1,0:T(8,128)} copy(f32[2,5,64,256]{2,3,1,0:T(8,128)} %get-tuple-element.52) | data formatting | bytes 1310720
  87.4 2.6 %copy.435 = f32[2,5,64,256]{3,2,1,0:T(8,128)} copy(f32[2,5,64,256]{2,3,1,0:T(8,128)} %get-tuple-element.53) | data formatting | bytes 1310720
  90.0 2.6 %copy.434 = f32[2,5,64,256]{3,2,1,0:T(8,128)} copy(f32[2,5,64,256]{2,3,1,0:T(8,128)} %get-tuple-element.54) | data formatting | bytes 1310720
  92.6 2.6 %copy.433 = f32[2,5,64,256]{3,2,1,0:T(8,128)} copy(f32[2,5,64,256]{2,3,1,0:T(8,128)} %get-tuple-element.51) | data formatting | bytes 1310720
  95.1 3.1 %pad_add_fusion = f32[2,9,64,256]{3,2,1,0:T(8,128)} fusion(f32[2,5,64,256]{3,2,1,0:T(8,128)S(1)} %copy.437, f32[2,5,64,256]{3,2,1,0:T(8,128)} %copy.436, f32[2,5,64,256]{3,2,1,0:T(8,128)} %copy.435, f32[2,5,64,256]{3,2,1,0:T(8,128)} %copy.434, f32[2,5,64,256]{3,2,1,0:T(8,128)} %copy.433), kind=kLoop, calls=%fused_computation.28 | loop fusion | flops 1179648 | bytes 4456448 | tf_op jit(solution)/shard_map/add | solution.py:61
  101.2 2.6 %convolution_multiply_fusion = f32[2,5,4,320,64]{3,4,2,1,0:T(8,128)} fusion(bf16[2,5,64,4,64]{2,4,3,1,0:T(8,128)(2,1)S(1)} %copy-done.23, bf16[2,5,4,64,320]{4,3,2,1,0:T(8,128)(2,1)S(1)} %copy-done.22), kind=kOutput, calls=%fused_computation.12 | convolution fusion | flops 105676800 | bytes 5242880 | tf_op jit(solution)/shard_map/abhqk,abqhd->abkhd/dot_general | solution.py:196
  103.8 1.7 %fusion.11 = bf16[2,5,64,4,64]{2,4,3,1,0:T(8,128)(2,1)} fusion(f32[2,5,64,4,64]{2,4,3,1,0:T(8,128)S(1)} %convolution_bitcast_fusion.2, bf16[2,5,320,4,64]{2,4,3,1,0:T(8,128)(2,1)S(1)} %concatenate.84, bf16[2,5,4,64,320]{4,3,2,1,0:T(8,128)(2,1)S(1)} %copy-done.22), kind=kOutput, calls=%fused_computation.21 | convolution fusion | flops 105349120 | bytes 4259840 | tf_op jit(solution)/shard_map/abhqk,abkhd->abqhd/dot_general | solution.py:167
  106.3 6.2 %fusion.69 = (f32[2,5,64,256]{2,3,1,0:T(8,128)}, f32[2,5,64,256]{2,3,1,0:T(8,128)S(1)}, f32[2,5,64,256]{2,3,1,0:T(8,128)}, f32[2,5,64,256]{2,3,1,0:T(8,128)}, f32[2,5,64,256]{2,3,1,0:T(8,128)}) fusion(f32[2,5,320,256]{2,3,1,0:T(8,128)} %bitcast.183), kind=kLoop, calls=%fused_computation.135 | loop fusion | bytes 6553600 | tf_op jit(solution)/shard_map/slice | solution.py:59
  112.5 1.7 %copy.432 = f32[2,5,64,256]{3,2,1,0:T(8,128)S(1)} copy(f32[2,5,64,256]{2,3,1,0:T(8,128)} %get-tuple-element.60) | data formatting | bytes 1310720
  114.6 1.9 %copy.430 = f32[2,5,64,256]{3,2,1,0:T(8,128)S(1)} copy(f32[2,5,64,256]{2,3,1,0:T(8,128)} %get-tuple-element.58) | data formatting | bytes 1310720
  116.5 1.9 %copy.429 = f32[2,5,64,256]{3,2,1,0:T(8,128)S(1)} copy(f32[2,5,64,256]{2,3,1,0:T(8,128)} %get-tuple-element.59) | data formatting | bytes 1310720
  118.5 2.8 %copy.428 = f32[2,5,64,256]{3,2,1,0:T(8,128)} copy(f32[2,5,64,256]{2,3,1,0:T(8,128)} %get-tuple-element.56) | data formatting | bytes 1310720
  121.3 2.4 %pad_add_fusion.1 = f32[2,9,64,256]{3,2,1,0:T(8,128)} fusion(f32[2,5,64,256]{3,2,1,0:T(8,128)S(1)} %copy.432, f32[2,5,64,256]{3,2,1,0:T(8,128)S(1)} %copy.431, f32[2,5,64,256]{3,2,1,0:T(8,128)S(1)} %copy.430, f32[2,5,64,256]{3,2,1,0:T(8,128)S(1)} %copy.429, f32[2,5,64,256]{3,2,1,0:T(8,128)} %copy.428), kind=kLoop, calls=%fused_computation.29 | loop fusion | flops 1179648 | bytes 4456448 | tf_op jit(solution)/shard_map/add | solution.py:61
  127.2 2.1 %slice.319 = f32[2,5,64,256]{3,2,1,0:T(8,128)} slice(f32[2,9,64,256]{3,2,1,0:T(8,128)} %pad_add_fusion), slice={[0:2], [2:7], [0:64], [0:256]} | slice | bytes 1310720 | tf_op jit(solution)/shard_map/slice | solution.py:212
  129.3 4.8 %collective-permute-start.9 = (f32[2,2,64,256]{3,2,1,0:T(8,128)}, f32[2,2,64,256]{3,2,1,0:T(8,128)S(1)}, u32[]{:S(2)}, u32[]{:S(2)}) collective-permute-start(f32[2,2,64,256]{3,2,1,0:T(8,128)} %get-tuple-element.61), channel_id=1, source_target_pairs={{8,0},{16,8},{24,16},{32,24},{40,32},{48,40},{56,48},{64,56},{72,6... | collective-permute-start | bytes 786440 | tf_op jit(solution)/shard_map/ppermute | solution.py:21
  134.1 4.8 %collective-permute-start.7 = (f32[2,2,64,256]{3,2,1,0:T(8,128)}, f32[2,2,64,256]{3,2,1,0:T(8,128)}, u32[]{:S(2)}, u32[]{:S(2)}) collective-permute-start(f32[2,2,64,256]{3,2,1,0:T(8,128)} %get-tuple-element.63), channel_id=1, source_target_pairs={{8,0},{16,8},{24,16},{32,24},{40,32},{48,40},{56,48},{64,56},{72,6... | collective-permute-start | bytes 786440 | tf_op jit(solution)/shard_map/ppermute | solution.py:21
  141.2 1.9 %fusion.36 = f32[2,5,64,256]{3,2,1,0:T(8,128)} fusion(f32[2,5,64,256]{3,2,1,0:T(8,128)} %slice.319, f32[2,2,64,256]{3,2,1,0:T(8,128)} %collective-permute-done.8, f32[2,5,64,256]{3,2,1,0:T(8,128)S(1)} %copy.437, f32[2,5,64,256]{3,2,1,0:T(8,128)S(1)} %copy-done.3, f32[2,5,64,256]{3,2,1,0:T(8,128)S(1)} %copy-done.5, f32[2,5,64,256]{3,2,1,0:T(8,128)S(1)} %copy-done.7, ...), kind=kLoop, calls=%fused_computation.76 | loop fusion | flops 327680 | bytes 3801088 | tf_op jit(solution)/shard_map/scatter-add | solution.py:212
  143.1 2.1 %collective-permute-done.6 = f32[2,2,64,256]{3,2,1,0:T(8,128)} collective-permute-done((f32[2,2,64,256]{3,2,1,0:T(8,128)}, f32[2,2,64,256]{3,2,1,0:T(8,128)}, u32[]{:S(2)}, u32[]{:S(2)}) %collective-permute-start.6) | collective-permute-done | bytes 262176 | tf_op jit(solution)/shard_map/ppermute | solution.py:19
  (174 shorter events, 41.5 us)
Async XLA Ops:
  7.2 25.3 %copy-start.30 = (bf16[16,40,256]{2,1,0:T(8,128)(2,1)S(1)}, bf16[16,40,256]{2,1,0:T(8,128)(2,1)}, u32[]{:S(2)}) copy-start(bf16[16,40,256]{2,1,0:T(8,128)(2,1)} %param.15) | copy-start | bytes 983044
  12.1 20.7 %all-to-all-start = ((bf16[2,8,2,256]{3,1,2,0:T(8,128)(2,1)}), bf16[2,8,2,256]{3,1,2,0:T(8,128)(2,1)S(1)}, u32[]{:S(2)}, u32[]{:S(2)}) async-start(bf16[2,8,2,256]{3,1,2,0:T(8,128)(2,1)} %pad_maximum_fusion.4), calls=%async_computation | async-start | bytes 32768 | tf_op jit(solution)/shard_map/all_to_all | solution.py:95
  18.5 120.3 %reduce-scatter.4.cloned.1.call-start = ((), (), s32[]{:S(2)}) async-start(), calls=%async_computation.2 | async-start | bytes 24576
  18.6 15.0 %copy-start.32 = (s32[2,5]{1,0:T(2,128)S(1)}, s32[2,5]{1,0:T(2,128)}, u32[]{:S(2)}) copy-start(s32[2,5]{1,0:T(2,128)} %param.20) | copy-start | bytes 124
  18.7 21.8 %collective-permute-start.2 = (s32[2,2,64]{2,0,1:T(2,128)S(1)}, s32[2,2,64]{2,0,1:T(2,128)S(1)}, u32[]{:S(2)}, u32[]{:S(2)}) collective-permute-start(s32[2,2,64]{2,0,1:T(2,128)S(1)} %get-tuple-element.97), channel_id=1, source_target_pairs={{0,8},{8,16},{16,24},{24,32},{32,40},{40,48},{48,56},{56,64},{64,7... | collective-permute-start | bytes 3080 | tf_op jit(solution)/shard_map/ppermute | solution.py:19
  18.8 21.7 %collective-permute-start.3 = (s32[2,2,64]{2,0,1:T(2,128)S(1)}, s32[2,2,64]{2,0,1:T(2,128)S(1)}, u32[]{:S(2)}, u32[]{:S(2)}) collective-permute-start(s32[2,2,64]{2,0,1:T(2,128)S(1)} %get-tuple-element.96), channel_id=1, source_target_pairs={{8,0},{16,8},{24,16},{32,24},{40,32},{48,40},{56,48},{64,56},{72,6... | collective-permute-start | bytes 3080 | tf_op jit(solution)/shard_map/ppermute | solution.py:21
  25.6 15.2 %collective-permute-start.1 = (bf16[2,2,64,256]{3,2,1,0:T(8,128)(2,1)}, bf16[2,2,64,256]{3,2,1,0:T(8,128)(2,1)}, u32[]{:S(2)}, u32[]{:S(2)}) collective-permute-start(bf16[2,2,64,256]{3,2,1,0:T(8,128)(2,1)} %get-tuple-element.83), channel_id=1, source_target_pairs={{8,0},{16,8},{24,16},{32,24},{40,32},{48,40},{56,48},{64,56},{72,6... | collective-permute-start | bytes 393224 | tf_op jit(solution)/shard_map/ppermute | solution.py:21
  27.0 13.8 %collective-permute-start = (bf16[2,2,64,256]{3,2,1,0:T(8,128)(2,1)}, bf16[2,2,64,256]{3,2,1,0:T(8,128)(2,1)}, u32[]{:S(2)}, u32[]{:S(2)}) collective-permute-start(bf16[2,2,64,256]{3,2,1,0:T(8,128)(2,1)} %get-tuple-element.84), channel_id=1, source_target_pairs={{0,8},{8,16},{16,24},{24,32},{32,40},{40,48},{48,56},{56,64},{64,7... | collective-permute-start | bytes 393224 | tf_op jit(solution)/shard_map/ppermute | solution.py:19
  27.7 26.6 %collective-permute-start.5 = (bf16[2,2,64,256]{3,2,1,0:T(8,128)(2,1)}, bf16[2,2,64,256]{3,2,1,0:T(8,128)(2,1)}, u32[]{:S(2)}, u32[]{:S(2)}) collective-permute-start(bf16[2,2,64,256]{3,2,1,0:T(8,128)(2,1)} %get-tuple-element.77), channel_id=1, source_target_pairs={{8,0},{16,8},{24,16},{32,24},{40,32},{48,40},{56,48},{64,56},{72,6... | collective-permute-start | bytes 393224 | tf_op jit(solution)/shard_map/ppermute | solution.py:21
  33.6 30.3 %copy-start.20 = (f32[2,5,4,64,16]{3,4,1,0,2:T(8,128)}, f32[2,5,4,64,16]{3,4,1,0,2:T(8,128)S(1)}, u32[]{:S(2)}) copy-start(f32[2,5,4,64,16]{3,4,1,0,2:T(8,128)S(1)} %get-tuple-element.103) | copy-start | bytes 491524
  40.5 13.9 %collective-permute-start.4 = (bf16[2,2,64,256]{3,2,1,0:T(8,128)(2,1)S(1)}, bf16[2,2,64,256]{3,2,1,0:T(8,128)(2,1)}, u32[]{:S(2)}, u32[]{:S(2)}) collective-permute-start(bf16[2,2,64,256]{3,2,1,0:T(8,128)(2,1)S(1)} %get-tuple-element.78), channel_id=1, source_target_pairs={{0,8},{8,16},{16,24},{24,32},{32,40},{40,48},{48,56},{56,64},{64,7... | collective-permute-start | bytes 393224 | tf_op jit(solution)/shard_map/ppermute | solution.py:19
  56.5 6.3 %copy-start.29 = (bf16[2,5,64,256]{3,2,1,0:T(8,128)(2,1)S(1)}, bf16[2,5,64,256]{3,2,1,0:T(8,128)(2,1)}, u32[]{:S(2)}) copy-start(bf16[2,5,64,256]{3,2,1,0:T(8,128)(2,1)} %get-tuple-element.67) | copy-start | bytes 983044
  65.4 5.3 %copy-start.27 = (bf16[2,5,64,4,64]{2,4,3,1,0:T(8,128)(2,1)S(1)}, bf16[2,5,64,4,64]{2,4,3,1,0:T(8,128)(2,1)}, u32[]{:S(2)}) copy-start(bf16[2,5,64,4,64]{2,4,3,1,0:T(8,128)(2,1)} %copy.376) | copy-start | bytes 983044
  70.6 4.6 %copy-start.1 = (f32[2,5,4,320,64]{3,4,2,1,0:T(8,128)S(1)}, f32[2,5,4,320,64]{3,4,2,1,0:T(8,128)}, u32[]{:S(2)}) copy-start(f32[2,5,4,320,64]{3,4,2,1,0:T(8,128)} %copy-done) | copy-start | bytes 9830404
  70.6 4.9 %copy-start.28 = (bf16[2,5,320,4,64]{2,4,3,1,0:T(8,128)(2,1)S(1)}, bf16[2,5,320,4,64]{2,4,3,1,0:T(8,128)(2,1)}, u32[]{:S(2)}) copy-start(bf16[2,5,320,4,64]{2,4,3,1,0:T(8,128)(2,1)} %concatenate.95) | copy-start | bytes 4915204
  114.2 9.5 %copy-start.10 = (f32[2,5,64,256]{3,2,1,0:T(8,128)}, f32[2,5,64,256]{3,2,1,0:T(8,128)S(1)}, u32[]{:S(2)}) copy-start(f32[2,5,64,256]{3,2,1,0:T(8,128)S(1)} %copy.432) | copy-start | bytes 1966084
  114.6 9.1 %copy-start.12 = (f32[2,5,64,256]{3,2,1,0:T(8,128)}, f32[2,5,64,256]{3,2,1,0:T(8,128)S(1)}, u32[]{:S(2)}) copy-start(f32[2,5,64,256]{3,2,1,0:T(8,128)S(1)} %copy.431) | copy-start | bytes 1966084
  116.5 7.2 %copy-start.14 = (f32[2,5,64,256]{3,2,1,0:T(8,128)}, f32[2,5,64,256]{3,2,1,0:T(8,128)S(1)}, u32[]{:S(2)}) copy-start(f32[2,5,64,256]{3,2,1,0:T(8,128)S(1)} %copy.430) | copy-start | bytes 1966084
  118.5 5.2 %copy-start.16 = (f32[2,5,64,256]{3,2,1,0:T(8,128)}, f32[2,5,64,256]{3,2,1,0:T(8,128)S(1)}, u32[]{:S(2)}) copy-start(f32[2,5,64,256]{3,2,1,0:T(8,128)S(1)} %copy.429) | copy-start | bytes 1966084
  126.0 13.7 %copy-start.31 = (s32[2,5]{1,0:T(2,128)S(1)}, s32[2,5]{1,0:T(2,128)}, u32[]{:S(2)}) copy-start(s32[2,5]{1,0:T(2,128)} %param.21) | copy-start | bytes 124
  127.2 14.0 %copy-start.3 = (f32[2,5,64,256]{3,2,1,0:T(8,128)S(1)}, f32[2,5,64,256]{3,2,1,0:T(8,128)}, u32[]{:S(2)}) copy-start(f32[2,5,64,256]{3,2,1,0:T(8,128)} %copy.436) | copy-start | bytes 1966084
  127.2 14.0 %copy-start.5 = (f32[2,5,64,256]{3,2,1,0:T(8,128)S(1)}, f32[2,5,64,256]{3,2,1,0:T(8,128)}, u32[]{:S(2)}) copy-start(f32[2,5,64,256]{3,2,1,0:T(8,128)} %copy.435) | copy-start | bytes 1966084
  127.2 14.0 %copy-start.7 = (f32[2,5,64,256]{3,2,1,0:T(8,128)S(1)}, f32[2,5,64,256]{3,2,1,0:T(8,128)}, u32[]{:S(2)}) copy-start(f32[2,5,64,256]{3,2,1,0:T(8,128)} %copy.434) | copy-start | bytes 1966084
  127.2 14.0 %copy-start.9 = (f32[2,5,64,256]{3,2,1,0:T(8,128)S(1)}, f32[2,5,64,256]{3,2,1,0:T(8,128)}, u32[]{:S(2)}) copy-start(f32[2,5,64,256]{3,2,1,0:T(8,128)} %copy.433) | copy-start | bytes 1966084
  129.3 11.8 %collective-permute-start.8 = (f32[2,2,64,256]{3,2,1,0:T(8,128)}, f32[2,2,64,256]{3,2,1,0:T(8,128)}, u32[]{:S(2)}, u32[]{:S(2)}) collective-permute-start(f32[2,2,64,256]{3,2,1,0:T(8,128)} %get-tuple-element.62), channel_id=1, source_target_pairs={{0,8},{8,16},{16,24},{24,32},{32,40},{40,48},{48,56},{56,64},{64,7... | collective-permute-start | bytes 786440 | tf_op jit(solution)/shard_map/ppermute | solution.py:19
  129.3 16.9 %collective-permute-start.9 = (f32[2,2,64,256]{3,2,1,0:T(8,128)}, f32[2,2,64,256]{3,2,1,0:T(8,128)S(1)}, u32[]{:S(2)}, u32[]{:S(2)}) collective-permute-start(f32[2,2,64,256]{3,2,1,0:T(8,128)} %get-tuple-element.61), channel_id=1, source_target_pairs={{8,0},{16,8},{24,16},{32,24},{40,32},{48,40},{56,48},{64,56},{72,6... | collective-permute-start | bytes 786440 | tf_op jit(solution)/shard_map/ppermute | solution.py:21
  134.1 11.1 %collective-permute-start.6 = (f32[2,2,64,256]{3,2,1,0:T(8,128)}, f32[2,2,64,256]{3,2,1,0:T(8,128)}, u32[]{:S(2)}, u32[]{:S(2)}) collective-permute-start(f32[2,2,64,256]{3,2,1,0:T(8,128)} %get-tuple-element.64), channel_id=1, source_target_pairs={{0,8},{8,16},{16,24},{24,32},{32,40},{40,48},{48,56},{56,64},{64,7... | collective-permute-start | bytes 786440 | tf_op jit(solution)/shard_map/ppermute | solution.py:19
  134.1 12.2 %collective-permute-start.7 = (f32[2,2,64,256]{3,2,1,0:T(8,128)}, f32[2,2,64,256]{3,2,1,0:T(8,128)}, u32[]{:S(2)}, u32[]{:S(2)}) collective-permute-start(f32[2,2,64,256]{3,2,1,0:T(8,128)} %get-tuple-element.63), channel_id=1, source_target_pairs={{8,0},{16,8},{24,16},{32,24},{40,32},{48,40},{56,48},{64,56},{72,6... | collective-permute-start | bytes 786440 | tf_op jit(solution)/shard_map/ppermute | solution.py:21
  139.7 5.5 %slice-start = ((f32[2,9,64,256]{3,2,1,0:T(8,128)}), f32[2,5,64,256]{3,2,1,0:T(8,128)S(1)}, s32[]{:S(2)}) async-start(f32[2,9,64,256]{3,2,1,0:T(8,128)} %pad_add_fusion.1), calls=%async_computation.3 | async-start | bytes 1310720 | tf_op jit(solution)/shard_map/slice | solution.py:210
  141.1 4.1 %copy-start.11 = (f32[2,5,64,256]{3,2,1,0:T(8,128)S(1)}, f32[2,5,64,256]{3,2,1,0:T(8,128)}, u32[]{:S(2)}) copy-start(f32[2,5,64,256]{3,2,1,0:T(8,128)} %copy-done.10) | copy-start | bytes 1966084
  141.1 4.1 %copy-start.13 = (f32[2,5,64,256]{3,2,1,0:T(8,128)S(1)}, f32[2,5,64,256]{3,2,1,0:T(8,128)}, u32[]{:S(2)}) copy-start(f32[2,5,64,256]{3,2,1,0:T(8,128)} %copy-done.12) | copy-start | bytes 1966084
  141.1 4.1 %copy-start.15 = (f32[2,5,64,256]{3,2,1,0:T(8,128)S(1)}, f32[2,5,64,256]{3,2,1,0:T(8,128)}, u32[]{:S(2)}) copy-start(f32[2,5,64,256]{3,2,1,0:T(8,128)} %copy-done.14) | copy-start | bytes 1966084
  (14 other events, 36.3 us)
Sparse Core Ops, SparseCore 0:
  106.4 12.8 reduce-scatter.3
